TPU v7x, 32 devices: a whole 2x2x4 slice. The times are simulated.
32 devices in a mesh: groups: 2 (over y), page: 4 (over z), tensor: 4 (over x, core).
Axes of the slice: x: 2, y: 2, z: 4, core: 2. Of those that a mesh axis runs over, the one named last changes fastest.
Arguments:
- query: bfloat16 [4096, 4096], P(('groups', 'page'), 'tensor'), parts along dimension 0, may hold values from -13 to 13
- memory: bfloat16 [2048, 1024], P(('groups', 'page'), 'tensor'), parts along dimension 0, may hold values from -20 to 20
- key_weight: bfloat16 [1024, 4096], P(None, 'tensor'), may hold values from -2.6 to 2.6
- value_weight: bfloat16 [1024, 4096], P(None, 'tensor'), may hold values from -0.1875 to 0.1875
- out_grad: bfloat16 [4096, 4096], P(('groups', 'page'), 'tensor'), parts along dimension 0, may hold values from -6 to 6
- mask_blocks: int32 [8, 3, 4, 2], P(('groups', 'page')), parts along dimension 0, may hold values from 0 to 1, as said below
Outputs:
- attended: bfloat16 [4096, 4096], P(('groups', 'page'), 'tensor'), parts along dimension 0
- query_grad: bfloat16 [4096, 4096], P(('groups', 'page'), 'tensor'), parts along dimension 0
- memory_grad: bfloat16 [2048, 1024], P(('groups', 'page'), 'tensor'), parts along dimension 0
There are 2 independent parts, one for each index of `groups`. A program takes and returns all parts, laid end to end along the dimension named above; an argument that names none is the same for every part. Nothing has to cross between parts.
Inputs may be any that keep to these rules, and one draw needn't show every extreme that they name: `mask_blocks`: for every page and every block of 128 query rows, at least one block of the page's own memory (slot 1) is marked.
All inputs are finite; a program needn't handle non-finite values.
Results may differ from a plain program's by a relative error of at most 0.02.
The roundings to bfloat16 on the way count: a program that leaves them out, or rounds other values in their place, can miss the bound.
Values may be sent and summed in bfloat16 or wider, within the bound.
A program may use at most 128 MiB of HBM per device.

v0:
```python
import math
import jax
import jax.numpy as jnp
from jax import lax
from jax.sharding import PartitionSpec as P

HD = 128
masked_score = -1e30


def padded(block, sides, width):
    for axis, dim in sides:
        count = lax.axis_size(axis)
        forward = [(i, i + 1) for i in range(count - 1)]
        backward = [(target, source) for source, target in forward]
        low = lax.ppermute(
            lax.slice_in_dim(block, block.shape[dim] - width, None, axis=dim), axis, forward
        )
        high = lax.ppermute(lax.slice_in_dim(block, 0, width, axis=dim), axis, backward)
        block = jnp.concatenate([low, block, high], axis=dim)
    return block


def from_behind(x, axis, by):
    devices = lax.axis_size(axis)
    pairs = [(i, i + by) for i in range(devices) if 0 <= i + by < devices]
    return lax.ppermute(x, axis, pairs)


def back_project(key_part, value_part, key_weight, value_weight):
    dims = (((1,), (1,)), ((), ()))
    return lax.dot_general(
        key_part, key_weight, dims, preferred_element_type=jnp.float32
    ) + lax.dot_general(value_part, value_weight, dims, preferred_element_type=jnp.float32)


def on_device(query, memory, key_weight, value_weight, out_grad, mask_blocks):
    token_rows = query.shape[0]
    features = query.shape[1]
    head_count = features // HD
    memory_rows = memory.shape[0]
    page_index = lax.axis_index("page")
    page_total = lax.axis_size("page")
    memory_rim = padded(memory, (("page", 0),), memory_rows)
    wide_memory = lax.all_gather(memory_rim, "tensor", axis=1, tiled=True)
    key_slab = jnp.dot(wide_memory, key_weight, preferred_element_type=jnp.float32).astype(
        jnp.bfloat16
    )
    value_slab = jnp.dot(wide_memory, value_weight, preferred_element_type=jnp.float32).astype(
        jnp.bfloat16
    )
    sources = page_index + jnp.arange(3, dtype=jnp.int32) - 1
    source_live = ((sources >= 0) & (sources < page_total)).astype(jnp.float32)
    block_grid = mask_blocks[0].astype(jnp.float32) * source_live[:, None, None]
    query_blocks = block_grid.shape[1]
    memory_blocks = block_grid.shape[2]
    block_size = token_rows // query_blocks
    spread_grid = jnp.transpose(block_grid, (1, 0, 2))[:, None, :, :, None]
    visible = jnp.broadcast_to(
        spread_grid, (query_blocks, block_size, 3, memory_blocks, block_size)
    ).reshape(token_rows, 3 * memory_rows)
    score_scale = 1.0 / math.sqrt(HD)
    query_heads = query.reshape(token_rows, head_count, HD)
    key_heads = key_slab.reshape(3 * memory_rows, head_count, HD)
    value_heads = value_slab.reshape(3 * memory_rows, head_count, HD)
    scores = (
        jnp.einsum("thd,khd->htk", query_heads, key_heads, preferred_element_type=jnp.float32)
        * score_scale
    )
    scores = jnp.where(visible[None] > 0, scores, masked_score)
    row_max = jnp.max(scores, axis=2, keepdims=True)
    exponent = jnp.exp(scores - row_max)
    weights = exponent / jnp.sum(exponent, axis=2, keepdims=True)
    rounded_weights = weights.astype(jnp.bfloat16)
    mixed = jnp.einsum(
        "htk,khd->thd", rounded_weights, value_heads, preferred_element_type=jnp.float32
    )
    attended = mixed.reshape(token_rows, features).astype(jnp.bfloat16)
    grad_rows = out_grad.reshape(token_rows, head_count, HD)
    weight_grad = jnp.einsum(
        "thd,khd->htk", grad_rows, value_heads, preferred_element_type=jnp.float32
    )
    row_inner = jnp.sum(weights * weight_grad, axis=2, keepdims=True)
    score_grad = (weights * (weight_grad - row_inner) * score_scale).astype(jnp.bfloat16)
    query_grad = jnp.einsum(
        "htk,khd->thd", score_grad, key_heads, preferred_element_type=jnp.float32
    )
    query_grad = query_grad.reshape(token_rows, features).astype(jnp.bfloat16)
    key_piece = jnp.einsum(
        "htk,thd->khd", score_grad, query_heads, preferred_element_type=jnp.float32
    )
    key_piece = key_piece.reshape(3 * memory_rows, features).astype(jnp.bfloat16)
    value_piece = jnp.einsum(
        "htk,thd->khd", rounded_weights, grad_rows, preferred_element_type=jnp.float32
    )
    value_piece = value_piece.reshape(3 * memory_rows, features).astype(jnp.bfloat16)
    toward_previous = jnp.stack([key_piece[:memory_rows], value_piece[:memory_rows]])
    toward_next = jnp.stack([key_piece[2 * memory_rows :], value_piece[2 * memory_rows :]])
    from_next = from_behind(toward_previous, "page", -1)
    from_prev = from_behind(toward_next, "page", 1)
    partial_value = back_project(
        key_piece[memory_rows : 2 * memory_rows],
        value_piece[memory_rows : 2 * memory_rows],
        key_weight,
        value_weight,
    )
    partial_value = partial_value + back_project(
        from_next[0], from_next[1], key_weight, value_weight
    )
    partial_value = partial_value + back_project(
        from_prev[0], from_prev[1], key_weight, value_weight
    )
    summed = lax.psum_scatter(
        partial_value.astype(jnp.bfloat16), "tensor", scatter_dimension=1, tiled=True
    )
    return (attended, query_grad, summed)


def solution(mesh):
    placed = (
        P(("groups", "page"), "tensor"),
        P(("groups", "page"), "tensor"),
        P(None, "tensor"),
        P(None, "tensor"),
        P(("groups", "page"), "tensor"),
        P(("groups", "page"), None, None, None),
    )
    return jax.shard_map(
        on_device,
        mesh=mesh,
        in_specs=placed,
        out_specs=(
            P(("groups", "page"), "tensor"),
            P(("groups", "page"), "tensor"),
            P(("groups", "page"), "tensor"),
        ),
        check_vma=False,
    )
```

profile of v0, /device:TPU:0, one launch (start us, length us, event | category | flops | bytes accessed | tf_op | source)
XLA Modules:
  0.0 164.3 jit_solution(5907997166472424290)
XLA Ops:
  7.2 0.0 copy-start
  7.2 0.0 all-gather.2.cloned.1.call-start
  7.2 1.4 collective-permute-start.1
  8.7 5.6 %collective-permute-start = (bf16[256,256]{1,0:T(8,128)(2,1)}, bf16[256,256]{1,0:T(8,128)(2,1)S(1)}, u32[]{:S(2)}, u32[]{:S(2)}) collective-permute-start(bf16[256,256]{1,0:T(8,128)(2,1)} %param.7), channel_id=1, source_target_pairs={{0,4},{4,8},{8,12},{1,5},{5,9},{9,13},{2,6},{6,10},{10,14},{3,7},{... | collective-permute-start | bytes 393224 | tf_op jit(solution)/shard_map/ppermute | solution.py:16
  14.2 1.8 %collective-permute-done.1 = bf16[256,256]{1,0:T(8,128)(2,1)S(1)} collective-permute-done((bf16[256,256]{1,0:T(8,128)(2,1)}, bf16[256,256]{1,0:T(8,128)(2,1)S(1)}, u32[]{:S(2)}, u32[]{:S(2)}) %collective-permute-start.1) | collective-permute-done | bytes 131104 | tf_op jit(solution)/shard_map/ppermute | solution.py:19
  16.0 1.3 collective-permute-done
  17.3 1.7 %pad_maximum_fusion.2 = bf16[768,256]{1,0:T(8,128)(2,1)} fusion(bf16[256,256]{1,0:T(8,128)(2,1)S(1)} %collective-permute-done.1, bf16[256,256]{1,0:T(8,128)(2,1)} %param.7, bf16[256,256]{1,0:T(8,128)(2,1)S(1)} %collective-permute-done), kind=kLoop, calls=%fused_computation.51 | loop fusion | flops 1179648 | bytes 786432 | tf_op jit(solution)/shard_map/concatenate | solution.py:20
  18.9 0.0 all-gather.2.cloned.1.call-update
  19.0 0.0 reduce-scatter.2.cloned.1.call-start
  19.0 0.8 compare_bitcast_fusion
  19.8 0.3 broadcast_in_dim.14
  20.1 0.2 copy.41
  20.3 2.3 %copy.28 = bf16[512,1024]{0,1:T(8,128)(2,1)} copy(bf16[512,1024]{1,0:T(8,128)(2,1)} %param.6) | data formatting | bytes 2097152 | tf_op jit(solution)/shard_map/reshape | solution.py:63
  22.6 1.5 copy.29
  24.1 17.2 %all-gather.2.cloned.1.call-done = bf16[768,1024]{1,0:T(8,128)(2,1)} async-done(((bf16[768,256]{1,0:T(8,128)(2,1)}), bf16[768,1024]{1,0:T(8,128)(2,1)}) %all-gather.2.cloned.1.call-update) | async-done | bytes 1572880 | tf_op jit(solution)/shard_map/all_gather | solution.py:45
  41.2 5.0 %convolution_convert_fusion = bf16[768,1024]{1,0:T(8,128)(2,1)} fusion(bf16[768,1024]{1,0:T(8,128)(2,1)} %all-gather.2.cloned.1.call-done, bf16[1024,1024]{1,0:T(8,128)(2,1)} %param.8), kind=kOutput, calls=%fused_computation.23 | convolution fusion | flops 1611399168 | bytes 5242880 | tf_op jit(solution)/shard_map/dot_general | solution.py:46
  46.3 2.6 %copy.27 = bf16[768,1024]{0,1:T(8,128)(2,1)} copy(bf16[768,1024]{1,0:T(8,128)(2,1)} %convolution_convert_fusion) | data formatting | bytes 3145728 | tf_op jit(solution)/shard_map/reshape | solution.py:64
  48.9 0.0 copy-done
  48.9 3.2 %fusion.26 = bf16[96,8,8,128]{3,2,1,0:T(8,128)(2,1)S(1)} fusion(bf16[768,1024]{1,0:T(8,128)(2,1)} %all-gather.2.cloned.1.call-done, bf16[1024,1024]{1,0:T(8,128)(2,1)S(1)} %copy-done), kind=kOutput, calls=%fused_computation.30 | convolution fusion | flops 1611399168 | bytes 5242880 | tf_op jit(solution)/shard_map/dot_general | solution.py:49
  52.1 0.0 copy-start.2
  52.1 6.3 %fusion.21 = f32[8,768,512]{2,1,0:T(8,128)} fusion(bf16[512,8,128]{0,2,1:T(8,128)(2,1)S(1)} %bitcast.118, bf16[96,8,8,128]{3,2,1,0:T(8,128)(2,1)S(1)} %fusion.26), kind=kOutput, calls=%fused_computation.26 | convolution fusion | flops 805306368 | bytes 15204352 | tf_op jit(solution)/shard_map/thd,khd->htk/dot_general | solution.py:80
  58.4 0.0 copy-done.2
  58.4 11.0 %fusion.51 = (f32[8,512]{1,0:T(8,128)S(1)}, f32[8,512,768]{1,2,0:T(8,128)}) fusion(pred[512,768]{0,1:T(8,128)(4,1)S(1)} %bitcast.133, bf16[768,8,128]{0,2,1:T(8,128)(2,1)} %bitcast.126, bf16[512,8,128]{0,2,1:T(8,128)(2,1)} %bitcast.129), kind=kOutput, calls=%fused_computation.63 | convolution fusion | flops 817890048 | bytes 15613952 | tf_op jit(solution)/shard_map/sub | solution.py:72
  69.4 8.0 %fusion.23 = bf16[768,8,128]{0,2,1:T(8,128)(2,1)} fusion(bf16[512,8,128]{0,2,1:T(8,128)(2,1)S(1)} %bitcast.119, f32[8,512,768]{1,2,0:T(8,128)} %get-tuple-element.13, f32[8,512]{1,0:T(8,128)S(1)} %get-tuple-element.12), kind=kOutput, calls=%fused_computation.29 | convolution fusion | flops 812384256 | bytes 15220736 | tf_op jit(solution)/shard_map/htk,thd->khd/dot_general | solution.py:93
  77.4 18.9 %fusion.27 = bf16[768,8,128]{0,2,1:T(8,128)(2,1)} fusion(bf16[512,8,128]{0,2,1:T(8,128)(2,1)} %bitcast.130, f32[8,768,512]{2,1,0:T(8,128)} %fusion.21, f32[8,512,768]{1,2,0:T(8,128)} %get-tuple-element.13, f32[8,512]{1,0:T(8,128)S(1)} %get-tuple-element.12), kind=kOutput, calls=%fused_computation.31 | convolution fusion | flops 828117760 | bytes 27803648 | tf_op jit(solution)/shard_map/htk,thd->khd/dot_general | solution.py:89
  96.3 0.0 copy-start.3
  96.3 1.6 fusion.49
  97.9 0.3 copy-done.3
  98.2 0.0 copy-start.1
  98.2 0.2 fusion.50
  98.4 0.1 pad_maximum_fusion
  98.5 1.4 collective-permute-start.2
  99.9 0.1 pad_maximum_fusion.1
  100.0 4.6 %collective-permute-start.3 = (bf16[2,256,1024]{1,2,0:T(8,128)(2,1)S(1)}, bf16[2,256,1024]{1,2,0:T(8,128)(2,1)S(1)}, u32[]{:S(2)}, u32[]{:S(2)}) collective-permute-start(bf16[2,256,1024]{1,2,0:T(8,128)(2,1)S(1)} %pad_maximum_fusion.1), channel_id=1, source_target_pairs={{0,4},{4,8},{8,12},{1,5},{5,9},{9,13},{2,6},{6,10},{10,14},{3,7},{... | collective-permute-start | bytes 3145736 | tf_op jit(solution)/shard_map/ppermute | solution.py:27
  104.6 0.0 copy-done.1
  104.6 0.8 fusion.52
  105.4 0.8 convolution_add_fusion.2
  106.2 19.6 %collective-permute-done.2 = bf16[2,256,1024]{1,2,0:T(8,128)(2,1)S(1)} collective-permute-done((bf16[2,256,1024]{1,2,0:T(8,128)(2,1)S(1)}, bf16[2,256,1024]{1,2,0:T(8,128)(2,1)S(1)}, u32[]{:S(2)}, u32[]{:S(2)}) %collective-permute-start.2) | collective-permute-done | bytes 1048608 | tf_op jit(solution)/shard_map/ppermute | solution.py:27
  125.8 0.8 fusion.42
  126.6 0.5 collective-permute-done.3
  127.1 0.8 fusion.41
  127.9 0.8 fusion.37
  128.7 1.6 fusion.38
  130.2 0.0 reduce-scatter.2.cloned.1.call-update
  130.3 6.3 %fusion.28 = bf16[8,128,512]{2,1,0:T(8,128)(2,1)S(1)} fusion(bf16[96,8,8,128]{3,2,1,0:T(8,128)(2,1)} %copy-done.2, f32[8,512,768]{1,2,0:T(8,128)} %get-tuple-element.13, f32[8,512]{1,0:T(8,128)S(1)} %get-tuple-element.12), kind=kOutput, calls=%fused_computation.32 | convolution fusion | flops 812122112 | bytes 15220736 | tf_op jit(solution)/shard_map/htk,khd->thd/dot_general | solution.py:75
  136.6 1.3 copy.21
  137.9 18.3 %fusion.33 = bf16[8,128,512]{2,1,0:T(8,128)(2,1)S(1)} fusion(bf16[768,8,128]{0,2,1:T(8,128)(2,1)} %bitcast.127, f32[8,768,512]{2,1,0:T(8,128)} %fusion.21, f32[8,512,768]{1,2,0:T(8,128)} %get-tuple-element.13, f32[8,512]{1,0:T(8,128)S(1)} %get-tuple-element.12), kind=kOutput, calls=%fused_computation.33 | convolution fusion | flops 827855616 | bytes 27803648 | tf_op jit(solution)/shard_map/htk,khd->thd/dot_general | solution.py:85
  156.1 1.3 copy.22
  (2 shorter events, 0.0 us)
Async XLA Ops:
  7.2 41.8 %copy-start = (bf16[1024,1024]{1,0:T(8,128)(2,1)S(1)}, bf16[1024,1024]{1,0:T(8,128)(2,1)}, u32[]{:S(2)}) copy-start(bf16[1024,1024]{1,0:T(8,128)(2,1)} %param.9) | copy-start | bytes 6291460
  7.2 34.1 %all-gather.2.cloned.1.call-start = ((), (), s32[]{:S(2)}) async-start(), calls=%async_computation.1 | async-start | bytes 1966080 | tf_op jit(solution)/shard_map/all_gather | solution.py:45
  7.2 8.8 %collective-permute-start.1 = (bf16[256,256]{1,0:T(8,128)(2,1)}, bf16[256,256]{1,0:T(8,128)(2,1)S(1)}, u32[]{:S(2)}, u32[]{:S(2)}) collective-permute-start(bf16[256,256]{1,0:T(8,128)(2,1)} %param.7), channel_id=1, source_target_pairs={{4,0},{8,4},{12,8},{5,1},{9,5},{13,9},{6,2},{10,6},{14,10},{7,3},{... | collective-permute-start | bytes 393224 | tf_op jit(solution)/shard_map/ppermute | solution.py:19
  8.7 8.6 %collective-permute-start = (bf16[256,256]{1,0:T(8,128)(2,1)}, bf16[256,256]{1,0:T(8,128)(2,1)S(1)}, u32[]{:S(2)}, u32[]{:S(2)}) collective-permute-start(bf16[256,256]{1,0:T(8,128)(2,1)} %param.7), channel_id=1, source_target_pairs={{0,4},{4,8},{8,12},{1,5},{5,9},{9,13},{2,6},{6,10},{10,14},{3,7},{... | collective-permute-start | bytes 393224 | tf_op jit(solution)/shard_map/ppermute | solution.py:16
  19.0 138.5 %reduce-scatter.2.cloned.1.call-start = ((), (), s32[]{:S(2)}) async-start(), calls=%async_computation.2 | async-start | bytes 655360 | tf_op jit(solution)/shard_map/reduce_scatter | solution.py:113
  52.1 6.3 %copy-start.2 = (bf16[96,8,8,128]{3,2,1,0:T(8,128)(2,1)}, bf16[96,8,8,128]{3,2,1,0:T(8,128)(2,1)S(1)}, u32[]{:S(2)}) copy-start(bf16[96,8,8,128]{3,2,1,0:T(8,128)(2,1)S(1)} %fusion.26) | copy-start | bytes 4718596
  96.3 1.9 %copy-start.3 = (bf16[768,8,128]{0,2,1:T(8,128)(2,1)S(1)}, bf16[768,8,128]{0,2,1:T(8,128)(2,1)}, u32[]{:S(2)}) copy-start(bf16[768,8,128]{0,2,1:T(8,128)(2,1)} %fusion.23) | copy-start | bytes 4718596
  98.2 6.4 %copy-start.1 = (bf16[1024,1024]{1,0:T(8,128)(2,1)S(1)}, bf16[1024,1024]{1,0:T(8,128)(2,1)}, u32[]{:S(2)}) copy-start(bf16[1024,1024]{1,0:T(8,128)(2,1)} %param.8) | copy-start | bytes 6291460
  98.5 27.3 %collective-permute-start.2 = (bf16[2,256,1024]{1,2,0:T(8,128)(2,1)S(1)}, bf16[2,256,1024]{1,2,0:T(8,128)(2,1)S(1)}, u32[]{:S(2)}, u32[]{:S(2)}) collective-permute-start(bf16[2,256,1024]{1,2,0:T(8,128)(2,1)S(1)} %pad_maximum_fusion), channel_id=1, source_target_pairs={{4,0},{8,4},{12,8},{5,1},{9,5},{13,9},{6,2},{10,6},{14,10},{7,3},{... | collective-permute-start | bytes 3145736 | tf_op jit(solution)/shard_map/ppermute | solution.py:27
  100.0 27.1 %collective-permute-start.3 = (bf16[2,256,1024]{1,2,0:T(8,128)(2,1)S(1)}, bf16[2,256,1024]{1,2,0:T(8,128)(2,1)S(1)}, u32[]{:S(2)}, u32[]{:S(2)}) collective-permute-start(bf16[2,256,1024]{1,2,0:T(8,128)(2,1)S(1)} %pad_maximum_fusion.1), channel_id=1, source_target_pairs={{0,4},{4,8},{8,12},{1,5},{5,9},{9,13},{2,6},{6,10},{10,14},{3,7},{... | collective-permute-start | bytes 3145736 | tf_op jit(solution)/shard_map/ppermute | solution.py:27
Sparse Core Ops, SparseCore 0:
  19.1 22.1 all-gather.1
  130.4 22.8 reduce-scatter.1
where the time goes:
time: 165 us; the launch traced here: 164 us
  matrix products  82.4 us (50%)
  waiting for transfers between devices  40.4 us (24%)
  between operations  14.2 us (9%)
  starting transfers between devices  13.1 us (8%)
  local copies, waits for them, and re-layouts  11.6 us (7%)
  other arithmetic  2.64 us (2%)
    ppermute x2, waiting for transfers between devices, from_behind(): return lax.ppermute(x, axis, pairs)  20.1 us
    dot_general x1, matrix products, on_device(): jnp.einsum('htk,thd->khd', score_grad, query_heads, preferred_element_typ...  18.9 us
    dot_general x1, matrix products, on_device(): jnp.einsum('htk,khd->thd', score_grad, key_heads, preferred_element_type=...  18.3 us
    all_gather x1, waiting for transfers between devices, on_device(): wide_memory = lax.all_gather(memory_rim, 'tensor', axis=1, tiled=True)  17.2 us
    sub x1, matrix products, on_device(): exponent = jnp.exp(scores - row_max)  11 us
    dot_general x1, matrix products, on_device(): jnp.einsum('htk,thd->khd', rounded_weights, grad_rows, preferred_element_...  7.97 us
    dot_general x1, matrix products, on_device(): jnp.einsum('htk,khd->thd', rounded_weights, value_heads, preferred_elemen...  6.29 us
    dot_general x1, matrix products, on_device(): jnp.einsum('thd,khd->htk', grad_rows, value_heads, preferred_element_type...  6.26 us
  transfers between devices with their start and end apart: 6, of which 5 were waited for; matrix products, arithmetic and copies ran while one was open for 21% of the time, Pallas kernels for 0%

commit v1 on v0

--- a/solution.py
+++ b/solution.py
@@ -6,6 +6,12 @@
 
 HD = 128
 masked_score = -1e30
+
+
+def joined_along(pieces, dim):
+    shape = list(pieces.shape[1:])
+    shape[dim] *= pieces.shape[0]
+    return jnp.moveaxis(pieces, 0, dim).reshape(shape)
 
 
 def padded(block, sides, width):
@@ -42,7 +48,19 @@
     page_index = lax.axis_index("page")
     page_total = lax.axis_size("page")
     memory_rim = padded(memory, (("page", 0),), memory_rows)
-    wide_memory = lax.all_gather(memory_rim, "tensor", axis=1, tiled=True)
+    length = lax.axis_size("tensor")
+    pairs_2 = [(i_2, (i_2 + 1) % length) for i_2 in range(length)]
+    back = [(b, a) for a, b in pairs_2]
+    lower, upper = ([], [])
+    for step in range(length - 1):
+        if step % 2 == 0:
+            lower.append(lax.ppermute(lower[-1] if lower else memory_rim, "tensor", pairs_2))
+        else:
+            upper.append(lax.ppermute(upper[-1] if upper else memory_rim, "tensor", back))
+    blocks = jnp.stack([*lower[::-1], memory_rim, *upper])
+    shift = lax.axis_index("tensor") - len(lower)
+    blocks = blocks[(jnp.arange(length) - shift) % length]
+    wide_memory = joined_along(blocks, 1)
     key_slab = jnp.dot(wide_memory, key_weight, preferred_element_type=jnp.float32).astype(
         jnp.bfloat16
     )

time: 165 us -> 169 us (1.024)
  local copies, waits for them, and re-layouts: 11.6 us -> 18.1 us
  waiting for transfers between devices: 40.4 us -> 35.2 us
    all_gather x1 -> x0, waiting for transfers between devices: 17.2 us -> none  [on_device(): wide_memory = lax.all_gather(memory_rim, 'tensor', axis=1, tiled=True)]
    ppermute x0 -> x3, waiting for transfers between devices: none -> 10.5 us  [the longest x2 10.5 us: on_device(): lax.ppermute(lower[-1] if lower else memory_rim, 'tensor', pairs_2)]
    gather x0 -> x1, local copies, waits for them, and re-layouts: none -> 3.2 us  [on_device(): blocks = blocks[(jnp.arange(length) - shift) % length]]
    transpose x0 -> x1, local copies, waits for them, and re-layouts: none -> 2.59 us  [joined_along(): return jnp.moveaxis(pieces, 0, dim).reshape(shape)]
    another operation x0 -> x1, other arithmetic: none -> 2.59 us  [on_device(): blocks = jnp.stack([*lower[::-1], memory_rim, *upper])]
    dot_general x1, matrix products: 5.02 us -> 3 us  [on_device(): jnp.dot(wide_memory, key_weight, preferred_element_type=jnp.float32)]
    ppermute x0 -> x3, starting transfers between devices: none -> 1.85 us  [the longest x1 1.72 us: on_device(): lax.ppermute(upper[-1] if upper else memory_rim, 'tensor', back)]
    unnamed x11 -> x19, local copies, waits for them, and re-layouts: 3.13 us -> 4.82 us
  transfers between devices with their start and end apart: 6 -> 8, of which waited for: 5 -> 6; matrix products, arithmetic and copies ran while one was open for 21% -> 21% of each run, Pallas kernels for 0% -> 0%
where the time goes in v1:
time: 169 us
  matrix products  83.2 us (49%)
  waiting for transfers between devices  35.2 us (21%)
  local copies, waits for them, and re-layouts  18.1 us (11%)
  starting transfers between devices  14.6 us (9%)
  between operations  14.3 us (8%)
  other arithmetic  3.57 us (2%)
    ppermute x2, waiting for transfers between devices, from_behind(): return lax.ppermute(x, axis, pairs)  19.8 us
    dot_general x1, matrix products, on_device(): jnp.einsum('htk,thd->khd', score_grad, query_heads, preferred_element_typ...  18.9 us
    dot_general x1, matrix products, on_device(): jnp.einsum('htk,khd->thd', score_grad, key_heads, preferred_element_type=...  18.3 us
    sub x1, matrix products, on_device(): exponent = jnp.exp(scores - row_max)  11 us
    ppermute x2, waiting for transfers between devices, on_device(): lax.ppermute(lower[-1] if lower else memory_rim, 'tensor', pairs_2)  10.5 us
    dot_general x1, matrix products, on_device(): jnp.einsum('htk,thd->khd', rounded_weights, grad_rows, preferred_element_...  7.97 us
    dot_general x1, matrix products, on_device(): jnp.einsum('thd,khd->htk', grad_rows, value_heads, preferred_element_type...  7.72 us
    dot_general x1, matrix products, on_device(): jnp.einsum('htk,khd->thd', rounded_weights, value_heads, preferred_elemen...  6.29 us
  transfers between devices with their start and end apart: 8, of which 6 were waited for; matrix products, arithmetic and copies ran while one was open for 21% of the time, Pallas kernels for 0%

profile of v1, /device:TPU:0, one launch (start us, length us, event | category | flops | bytes accessed | tf_op | source)
XLA Modules:
  0.0 168.9 jit_solution(17556644474784105043)
XLA Ops:
  7.2 0.0 copy-start
  7.2 0.0 reduce-scatter.2.cloned.1.call-start
  7.2 5.2 %collective-permute-start = (bf16[256,256]{1,0:T(8,128)(2,1)}, bf16[256,256]{1,0:T(8,128)(2,1)S(1)}, u32[]{:S(2)}, u32[]{:S(2)}) collective-permute-start(bf16[256,256]{1,0:T(8,128)(2,1)} %param.7), channel_id=1, source_target_pairs={{0,4},{4,8},{8,12},{1,5},{5,9},{9,13},{2,6},{6,10},{10,14},{3,7},{... | collective-permute-start | bytes 393224 | tf_op jit(solution)/shard_map/ppermute | solution.py:22
  12.4 1.3 collective-permute-start.1
  13.7 1.7 %collective-permute-done = bf16[256,256]{1,0:T(8,128)(2,1)S(1)} collective-permute-done((bf16[256,256]{1,0:T(8,128)(2,1)}, bf16[256,256]{1,0:T(8,128)(2,1)S(1)}, u32[]{:S(2)}, u32[]{:S(2)}) %collective-permute-start) | collective-permute-done | bytes 131104 | tf_op jit(solution)/shard_map/ppermute | solution.py:22
  15.5 0.9 constant_dynamic-update-slice_fusion.1
  16.4 3.1 %collective-permute-done.1 = bf16[256,256]{1,0:T(8,128)(2,1)S(1)} collective-permute-done((bf16[256,256]{1,0:T(8,128)(2,1)}, bf16[256,256]{1,0:T(8,128)(2,1)S(1)}, u32[]{:S(2)}, u32[]{:S(2)}) %collective-permute-start.1) | collective-permute-done | bytes 131104 | tf_op jit(solution)/shard_map/ppermute | solution.py:25
  19.5 0.1 collective-permute-start.2
  19.6 1.7 %collective-permute-start.4 = (bf16[768,256]{1,0:T(8,128)(2,1)S(1)}, bf16[768,256]{1,0:T(8,128)(2,1)}, u32[]{:S(2)}, u32[]{:S(2)}) collective-permute-start(bf16[768,256]{1,0:T(8,128)(2,1)S(1)} %constant_dynamic-update-slice_fusion), channel_id=1, source_target_pairs={{1,0},{2,1},{3,2},{0,3},{5,4},{6,5},{7,6},{4,7},{9,8},{10,9},{11,1... | collective-permute-start | bytes 1179656 | tf_op jit(solution)/shard_map/ppermute | solution.py:59
  21.3 7.9 %collective-permute-done.2 = bf16[768,256]{1,0:T(8,128)(2,1)} collective-permute-done((bf16[768,256]{1,0:T(8,128)(2,1)S(1)}, bf16[768,256]{1,0:T(8,128)(2,1)}, u32[]{:S(2)}, u32[]{:S(2)}) %collective-permute-start.2) | collective-permute-done | bytes 393248 | tf_op jit(solution)/shard_map/ppermute | solution.py:57
  29.2 0.1 collective-permute-start.3
  29.3 0.8 compare_bitcast_fusion
  30.1 0.3 broadcast_in_dim.14
  30.4 0.9 copy.70
  31.3 1.3 copy.57
  32.6 1.5 copy.58
  34.2 2.6 %collective-permute-done.3 = bf16[768,256]{1,0:T(8,128)(2,1)} collective-permute-done((bf16[768,256]{1,0:T(8,128)(2,1)}, bf16[768,256]{1,0:T(8,128)(2,1)}, u32[]{:S(2)}, u32[]{:S(2)}) %collective-permute-start.3) | collective-permute-done | bytes 393248 | tf_op jit(solution)/shard_map/ppermute | solution.py:57
  36.8 2.6 %pad_maximum_fusion = bf16[4,768,256]{2,1,0:T(8,128)(2,1)} fusion(bf16[1,768,256]{2,1,0:T(8,128)(2,1)} %bitcast.3, bf16[1,768,256]{2,1,0:T(8,128)(2,1)S(1)} %bitcast.144, bf16[1,768,256]{2,1,0:T(8,128)(2,1)} %bitcast.1, bf16[1,768,256]{2,1,0:T(8,128)(2,1)} %bitcast), kind=kLoop, calls=%fused_computation.29 | loop fusion | flops 2359296 | bytes 3145728 | tf_op jit(solution)/shard_map/stack | solution.py:60
  39.3 3.2 %gather_fusion = bf16[4,768,256]{2,1,0:T(8,128)(2,1)} fusion(bf16[4,768,256]{2,1,0:T(8,128)(2,1)} %pad_maximum_fusion, s32[1024]{0:T(1024)S(1)} %pad_clamp_fusion), kind=kCustom, calls=%fused_computation | custom fusion | bytes 3145744 | tf_op jit(solution)/shard_map/gather | solution.py:62
  42.5 2.6 %copy.37 = bf16[768,4,256]{0,2,1:T(8,128)(2,1)} copy(bf16[768,4,256]{2,0,1:T(8,128)(2,1)} %bitcast.126) | data formatting | bytes 3145728 | tf_op jit(solution)/shard_map/transpose | solution.py:14
  45.1 4.6 %fusion.26 = bf16[96,8,8,128]{3,2,1,0:T(8,128)(2,1)} fusion(bf16[768,1024]{0,1:T(8,128)(2,1)} %bitcast.137, bf16[1024,1024]{1,0:T(8,128)(2,1)S(1)} %copy-done), kind=kOutput, calls=%fused_computation.32 | convolution fusion | flops 1611399168 | bytes 5242880 | tf_op jit(solution)/shard_map/dot_general | solution.py:67
  49.8 3.0 %convolution_convert_fusion = bf16[768,1024]{1,0:T(8,128)(2,1)} fusion(bf16[768,1024]{0,1:T(8,128)(2,1)S(1)} %bitcast.138, bf16[1024,1024]{1,0:T(8,128)(2,1)S(1)} %copy-done.1), kind=kOutput, calls=%fused_computation.24 | convolution fusion | flops 1611399168 | bytes 5242880 | tf_op jit(solution)/shard_map/dot_general | solution.py:64
  52.8 2.6 %copy.56 = bf16[768,1024]{0,1:T(8,128)(2,1)} copy(bf16[768,1024]{1,0:T(8,128)(2,1)} %convolution_convert_fusion) | data formatting | bytes 3145728 | tf_op jit(solution)/shard_map/reshape | solution.py:82
  55.3 7.7 %fusion.21 = f32[8,768,512]{2,1,0:T(8,128)} fusion(bf16[512,8,128]{0,2,1:T(8,128)(2,1)S(1)} %bitcast.127, bf16[96,8,8,128]{3,2,1,0:T(8,128)(2,1)} %fusion.26), kind=kOutput, calls=%fused_computation.27 | convolution fusion | flops 805306368 | bytes 15204352 | tf_op jit(solution)/shard_map/thd,khd->htk/dot_general | solution.py:98
  63.1 11.0 %fusion.53 = (f32[8,512]{1,0:T(8,128)S(1)}, f32[8,512,768]{1,2,0:T(8,128)}) fusion(pred[512,768]{0,1:T(8,128)(4,1)S(1)} %bitcast.145, bf16[768,8,128]{0,2,1:T(8,128)(2,1)} %bitcast.135, bf16[512,8,128]{0,2,1:T(8,128)(2,1)} %bitcast.140), kind=kOutput, calls=%fused_computation.74 | convolution fusion | flops 817890048 | bytes 15613952 | tf_op jit(solution)/shard_map/sub | solution.py:90
  74.1 8.0 %fusion.23 = bf16[768,8,128]{0,2,1:T(8,128)(2,1)} fusion(bf16[512,8,128]{0,2,1:T(8,128)(2,1)S(1)} %bitcast.128, f32[8,512,768]{1,2,0:T(8,128)} %get-tuple-element.19, f32[8,512]{1,0:T(8,128)S(1)} %get-tuple-element.18), kind=kOutput, calls=%fused_computation.31 | convolution fusion | flops 812384256 | bytes 15220736 | tf_op jit(solution)/shard_map/htk,thd->khd/dot_general | solution.py:111
  82.1 18.9 %fusion.27 = bf16[768,8,128]{0,2,1:T(8,128)(2,1)} fusion(bf16[512,8,128]{0,2,1:T(8,128)(2,1)} %bitcast.141, f32[8,768,512]{2,1,0:T(8,128)} %fusion.21, f32[8,512,768]{1,2,0:T(8,128)} %get-tuple-element.19, f32[8,512]{1,0:T(8,128)S(1)} %get-tuple-element.18), kind=kOutput, calls=%fused_computation.33 | convolution fusion | flops 828117760 | bytes 27803648 | tf_op jit(solution)/shard_map/htk,thd->khd/dot_general | solution.py:107
  100.9 1.6 fusion.51
  102.6 0.3 copy-done.3
  102.8 0.2 fusion.52
  103.0 0.0 copy-start.2
  103.0 0.1 pad_maximum_fusion.1
  103.1 1.4 collective-permute-start.5
  104.6 0.1 pad_maximum_fusion.2
  104.7 4.8 %collective-permute-start.6 = (bf16[2,256,1024]{1,2,0:T(8,128)(2,1)S(1)}, bf16[2,256,1024]{1,2,0:T(8,128)(2,1)S(1)}, u32[]{:S(2)}, u32[]{:S(2)}) collective-permute-start(bf16[2,256,1024]{1,2,0:T(8,128)(2,1)S(1)} %pad_maximum_fusion.2), channel_id=1, source_target_pairs={{0,4},{4,8},{8,12},{1,5},{5,9},{9,13},{2,6},{6,10},{10,14},{3,7},{... | collective-permute-start | bytes 3145736 | tf_op jit(solution)/shard_map/ppermute | solution.py:33
  109.5 0.8 fusion.54
  110.3 0.8 convolution_add_fusion.2
  111.1 19.3 %collective-permute-done.5 = bf16[2,256,1024]{1,2,0:T(8,128)(2,1)S(1)} collective-permute-done((bf16[2,256,1024]{1,2,0:T(8,128)(2,1)S(1)}, bf16[2,256,1024]{1,2,0:T(8,128)(2,1)S(1)}, u32[]{:S(2)}, u32[]{:S(2)}) %collective-permute-start.5) | collective-permute-done | bytes 1048608 | tf_op jit(solution)/shard_map/ppermute | solution.py:33
  130.4 0.8 fusion.42
  131.2 0.5 collective-permute-done.6
  131.7 0.8 fusion.41
  132.5 0.8 fusion.37
  133.3 1.6 fusion.38
  134.8 0.0 reduce-scatter.2.cloned.1.call-update
  134.8 6.3 %fusion.28 = bf16[8,128,512]{2,1,0:T(8,128)(2,1)S(1)} fusion(bf16[96,8,8,128]{3,2,1,0:T(8,128)(2,1)} %fusion.26, f32[8,512,768]{1,2,0:T(8,128)} %get-tuple-element.19, f32[8,512]{1,0:T(8,128)S(1)} %get-tuple-element.18), kind=kOutput, calls=%fused_computation.34 | convolution fusion | flops 812122112 | bytes 15220736 | tf_op jit(solution)/shard_map/htk,khd->thd/dot_general | solution.py:93
  141.1 1.3 copy.50
  142.5 18.3 %fusion.33 = bf16[8,128,512]{2,1,0:T(8,128)(2,1)S(1)} fusion(bf16[768,8,128]{0,2,1:T(8,128)(2,1)} %bitcast.136, f32[8,768,512]{2,1,0:T(8,128)} %fusion.21, f32[8,512,768]{1,2,0:T(8,128)} %get-tuple-element.19, f32[8,512]{1,0:T(8,128)S(1)} %get-tuple-element.18), kind=kOutput, calls=%fused_computation.35 | convolution fusion | flops 827855616 | bytes 27803648 | tf_op jit(solution)/shard_map/htk,khd->thd/dot_general | solution.py:103
  160.7 1.3 copy.51
  (18 shorter events, 0.1 us)
Async XLA Ops:
  7.2 38.0 %copy-start = (bf16[1024,1024]{1,0:T(8,128)(2,1)S(1)}, bf16[1024,1024]{1,0:T(8,128)(2,1)}, u32[]{:S(2)}) copy-start(bf16[1024,1024]{1,0:T(8,128)(2,1)} %param.9) | copy-start | bytes 6291460
  7.2 24.1 %copy-start.5 = (bf16[512,1024]{1,0:T(8,128)(2,1)S(1)}, bf16[512,1024]{1,0:T(8,128)(2,1)}, u32[]{:S(2)}) copy-start(bf16[512,1024]{1,0:T(8,128)(2,1)} %param.6) | copy-start | bytes 3145732
  7.2 154.9 %reduce-scatter.2.cloned.1.call-start = ((), (), s32[]{:S(2)}) async-start(), calls=%async_computation.1 | async-start | bytes 655360 | tf_op jit(solution)/shard_map/reduce_scatter | solution.py:131
  7.2 8.3 %collective-permute-start = (bf16[256,256]{1,0:T(8,128)(2,1)}, bf16[256,256]{1,0:T(8,128)(2,1)S(1)}, u32[]{:S(2)}, u32[]{:S(2)}) collective-permute-start(bf16[256,256]{1,0:T(8,128)(2,1)} %param.7), channel_id=1, source_target_pairs={{0,4},{4,8},{8,12},{1,5},{5,9},{9,13},{2,6},{6,10},{10,14},{3,7},{... | collective-permute-start | bytes 393224 | tf_op jit(solution)/shard_map/ppermute | solution.py:22
  12.4 7.1 %collective-permute-start.1 = (bf16[256,256]{1,0:T(8,128)(2,1)}, bf16[256,256]{1,0:T(8,128)(2,1)S(1)}, u32[]{:S(2)}, u32[]{:S(2)}) collective-permute-start(bf16[256,256]{1,0:T(8,128)(2,1)} %param.7), channel_id=1, source_target_pairs={{4,0},{8,4},{12,8},{5,1},{9,5},{13,9},{6,2},{10,6},{14,10},{7,3},{... | collective-permute-start | bytes 393224 | tf_op jit(solution)/shard_map/ppermute | solution.py:25
  19.5 9.7 %collective-permute-start.2 = (bf16[768,256]{1,0:T(8,128)(2,1)S(1)}, bf16[768,256]{1,0:T(8,128)(2,1)}, u32[]{:S(2)}, u32[]{:S(2)}) collective-permute-start(bf16[768,256]{1,0:T(8,128)(2,1)S(1)} %constant_dynamic-update-slice_fusion), channel_id=1, source_target_pairs={{0,1},{1,2},{2,3},{3,0},{4,5},{5,6},{6,7},{7,4},{8,9},{9,10},{10,1... | collective-permute-start | bytes 1179656 | tf_op jit(solution)/shard_map/ppermute | solution.py:57
  19.6 14.5 %collective-permute-start.4 = (bf16[768,256]{1,0:T(8,128)(2,1)S(1)}, bf16[768,256]{1,0:T(8,128)(2,1)}, u32[]{:S(2)}, u32[]{:S(2)}) collective-permute-start(bf16[768,256]{1,0:T(8,128)(2,1)S(1)} %constant_dynamic-update-slice_fusion), channel_id=1, source_target_pairs={{1,0},{2,1},{3,2},{0,3},{5,4},{6,5},{7,6},{4,7},{9,8},{10,9},{11,1... | collective-permute-start | bytes 1179656 | tf_op jit(solution)/shard_map/ppermute | solution.py:59
  29.2 7.5 %collective-permute-start.3 = (bf16[768,256]{1,0:T(8,128)(2,1)}, bf16[768,256]{1,0:T(8,128)(2,1)}, u32[]{:S(2)}, u32[]{:S(2)}) collective-permute-start(bf16[768,256]{1,0:T(8,128)(2,1)} %collective-permute-done.2), channel_id=1, source_target_pairs={{0,1},{1,2},{2,3},{3,0},{4,5},{5,6},{6,7},{7,4},{8,9},{9,10},{10,1... | collective-permute-start | bytes 1179656 | tf_op jit(solution)/shard_map/ppermute | solution.py:57
  45.1 4.6 %copy-start.1 = (bf16[1024,1024]{1,0:T(8,128)(2,1)S(1)}, bf16[1024,1024]{1,0:T(8,128)(2,1)}, u32[]{:S(2)}) copy-start(bf16[1024,1024]{1,0:T(8,128)(2,1)} %param.8) | copy-start | bytes 6291460
  45.1 4.6 %copy-start.4 = (bf16[768,4,256]{0,2,1:T(8,128)(2,1)S(1)}, bf16[768,4,256]{0,2,1:T(8,128)(2,1)}, u32[]{:S(2)}) copy-start(bf16[768,4,256]{0,2,1:T(8,128)(2,1)} %copy.37) | copy-start | bytes 4718596
  55.3 7.7 %copy-start.6 = (pred[96,8,4,128]{3,1,2,0:T(8,128)(4,1)S(1)}, pred[96,8,4,128]{3,1,2,0:T(8,128)(4,1)}, u32[]{:S(2)}) copy-start(pred[96,8,4,128]{3,1,2,0:T(8,128)(4,1)} %copy.70) | copy-start | bytes 1179652
  100.9 1.9 %copy-start.3 = (bf16[768,8,128]{0,2,1:T(8,128)(2,1)S(1)}, bf16[768,8,128]{0,2,1:T(8,128)(2,1)}, u32[]{:S(2)}) copy-start(bf16[768,8,128]{0,2,1:T(8,128)(2,1)} %fusion.23) | copy-start | bytes 4718596
  103.0 6.5 %copy-start.2 = (bf16[1024,1024]{1,0:T(8,128)(2,1)S(1)}, bf16[1024,1024]{1,0:T(8,128)(2,1)}, u32[]{:S(2)}) copy-start(bf16[1024,1024]{1,0:T(8,128)(2,1)} %param.8) | copy-start | bytes 6291460
  103.1 27.3 %collective-permute-start.5 = (bf16[2,256,1024]{1,2,0:T(8,128)(2,1)S(1)}, bf16[2,256,1024]{1,2,0:T(8,128)(2,1)S(1)}, u32[]{:S(2)}, u32[]{:S(2)}) collective-permute-start(bf16[2,256,1024]{1,2,0:T(8,128)(2,1)S(1)} %pad_maximum_fusion.1), channel_id=1, source_target_pairs={{4,0},{8,4},{12,8},{5,1},{9,5},{13,9},{6,2},{10,6},{14,10},{7,3},{... | collective-permute-start | bytes 3145736 | tf_op jit(solution)/shard_map/ppermute | solution.py:33
  104.7 27.0 %collective-permute-start.6 = (bf16[2,256,1024]{1,2,0:T(8,128)(2,1)S(1)}, bf16[2,256,1024]{1,2,0:T(8,128)(2,1)S(1)}, u32[]{:S(2)}, u32[]{:S(2)}) collective-permute-start(bf16[2,256,1024]{1,2,0:T(8,128)(2,1)S(1)} %pad_maximum_fusion.2), channel_id=1, source_target_pairs={{0,4},{4,8},{8,12},{1,5},{5,9},{9,13},{2,6},{6,10},{10,14},{3,7},{... | collective-permute-start | bytes 3145736 | tf_op jit(solution)/shard_map/ppermute | solution.py:33
Sparse Core Ops, SparseCore 0:
  135.0 22.9 reduce-scatter.1
